TPU v7x, 128 devices: a whole 4x4x4 slice. The times are simulated.
128 devices in a mesh: fsdp: 32 (over y_lo, z, x), rep: 4 (over y_hi, core).
Axes of the slice: x: 4, y: 4 (y_hi: 2, y_lo: 2; y = y_hi * 2 + y_lo), z: 4, core: 2. Of those that a mesh axis runs over, the one named last changes fastest.
Arguments:
- weights: bfloat16 [16384, 32768], P(('fsdp', 'rep')), may hold values from -0.046875 to 0.046875
- exponents: int32 [128, 256], P(None, ('fsdp', 'rep')), may hold values from -10 to -5
Outputs:
- quantized: bfloat16 [16384, 32768], P(None, ('fsdp', 'rep'))
- peak: float32 [], replicated
All inputs are finite; a program needn't handle non-finite values.
Results may differ from a plain program's by a relative error of at most 0.015.
Values may be sent and summed in bfloat16 or wider, within the bound.
No kernel may reach another device: no remote copies, remote signals or barrier semaphores. Data moves between devices by JAX's collectives and lax.ppermute only.
A program may use at most 128 MiB of HBM per device.

v0:
```python
import math

import jax
import jax.numpy as jnp
from jax import lax
from jax.sharding import PartitionSpec as P

INNER = 128
OUTER = 128


low_power = -10
high_power = -5


def hadamard(length):
    indices = lax.iota(jnp.int32, length)
    anded = jnp.bitwise_and(indices[:, None], indices[None, :])
    parity = jnp.zeros((length, length), jnp.int32)
    for bit_place in range(length.bit_length()):
        parity = parity + anded // 2**bit_place % 2
    return (1 - 2 * (parity % 2)).astype(jnp.bfloat16)


def block_factor(exponents):
    factor = jnp.zeros(exponents.shape, jnp.float32)
    for exponent in range(low_power, high_power + 1):
        factor = jnp.where(exponents == exponent, jnp.float32(2.0 ** (-exponent)), factor)
    return factor


def on_device(weights, exponents):
    fsdp_count = lax.axis_size("fsdp")
    rep_count = lax.axis_size("rep")
    devices = fsdp_count * rep_count
    outer_local = weights.shape[0] // INNER
    total_cols = weights.shape[1]
    cols_dev = total_cols // devices
    inner_table = hadamard(INNER)
    outer_table = hadamard(OUTER)
    inner_norm = 1.0 / math.sqrt(INNER)
    outer_norm = 1.0 / math.sqrt(OUTER)
    source = weights.reshape(outer_local, INNER, total_cols)
    mixture = jnp.einsum("ij,ajc->aic", inner_table, source, preferred_element_type=jnp.float32)
    moving = (mixture * inner_norm).astype(jnp.bfloat16)
    packed = moving.reshape(1, outer_local, INNER, devices, cols_dev)
    received = lax.all_to_all(packed, ("fsdp", "rep"), split_axis=3, concat_axis=0, tiled=True)
    mixture = jnp.einsum(
        "pa,aic->pic",
        outer_table,
        received.reshape(OUTER, INNER, received.shape[-1]),
        preferred_element_type=jnp.float32,
    )
    rotated = mixture * outer_norm
    factor = jnp.repeat(block_factor(exponents), INNER, axis=1)[:, None, :]
    quantized = (rotated * factor).astype(jnp.bfloat16).reshape(OUTER * INNER, cols_dev)
    local_peak = jnp.max(jnp.abs(quantized.astype(jnp.float32)))
    overall_peak = lax.pmax(local_peak, ("fsdp", "rep"))
    return (quantized, overall_peak)


def solution(mesh):
    return jax.shard_map(
        on_device,
        mesh=mesh,
        in_specs=(P(("fsdp", "rep"), None), P(None, ("fsdp", "rep"))),
        out_specs=(P(None, ("fsdp", "rep")), P()),
        check_vma=False,
    )
```

profile of v0, /device:TPU:1, one launch (start us, length us, event | category | flops | bytes accessed | tf_op | source)
XLA Modules:
  0.0 243.5 jit_solution(7719131866586238045)
XLA Ops:
  0.6 9.4 %fusion = bf16[128,32768]{1,0:T(8,128)(2,1)} fusion(bf16[128,32768]{1,0:T(8,128)(2,1)} %param.2), kind=kOutput, calls=%fused_computation.1 | convolution fusion | flops 1085046784 | bytes 16777216 | tf_op jit(solution)/shard_map/ij,ajc->aic/dot_general | solution.py:44
  10.1 9.1 %copy.11 = bf16[16,8,128,256]{3,2,1,0:T(8,128)(2,1)} copy(bf16[16,8,128,256]{3,1,2,0:T(8,128)(2,1)} %bitcast.30) | data formatting | bytes 16777216
  19.1 11.5 %copy.7 = bf16[1,1,128,128,256]{4,2,1,0,3:T(8,128)(2,1)} copy(bf16[1,1,128,128,256]{4,3,2,1,0:T(8,128)(2,1)} %bitcast.29) | data formatting | bytes 16777216 | tf_op jit(solution)/shard_map/reshape | solution.py:46
  30.7 0.0 copy-start
  30.7 12.0 %all-to-all-start = ((bf16[1,1,128,128,256]{4,2,1,0,3:T(8,128)(2,1)}), bf16[1,1,128,128,256]{4,2,1,0,3:T(8,128)(2,1)}, u32[]{:S(2)}, u32[]{:S(2)}) async-start(bf16[1,1,128,128,256]{4,2,1,0,3:T(8,128)(2,1)} %copy.7), calls=%async_computation | async-start | bytes 16777216 | tf_op jit(solution)/shard_map/all_to_all | solution.py:47
  42.7 0.0 copy-done
  42.7 0.1 copy.9
  42.8 0.2 broadcast_in_dim.36
  43.0 104.5 %all-to-all-done = bf16[1,1,128,128,256]{4,2,1,0,3:T(8,128)(2,1)} async-done(((bf16[1,1,128,128,256]{4,2,1,0,3:T(8,128)(2,1)}), bf16[1,1,128,128,256]{4,2,1,0,3:T(8,128)(2,1)}, u32[]{:S(2)}, u32[]{:S(2)}) %all-to-all-start) | async-done | bytes 8388640 | tf_op jit(solution)/shard_map/all_to_all | solution.py:47
  147.6 17.6 %abs_reduce_fusion = (f32[]{:T(128)}, bf16[128,128,256]{2,0,1:T(8,128)(2,1)}) fusion(f32[128,256]{1,0:T(8,128)S(1)} %bitcast.33, bf16[1,1,128,128,256]{4,2,1,0,3:T(8,128)(2,1)} %all-to-all-done), kind=kOutput, calls=%fused_computation.2 | convolution fusion | flops 1097629696 | bytes 16908292 | tf_op jit(solution)/shard_map/pa,aic->pic/dot_general | solution.py:48
  165.2 11.5 %copy.10 = bf16[128,128,256]{2,1,0:T(8,128)(2,1)} copy(bf16[128,128,256]{2,0,1:T(8,128)(2,1)} %get-tuple-element.3) | data formatting | bytes 16777216 | tf_op jit(solution)/shard_map/convert_element_type | solution.py:56
  176.7 66.8 %pmax.7 = f32[]{:T(128)} all-reduce(f32[]{:T(128)} %get-tuple-element.2), channel_id=1, replica_groups=mesh['fsdp'=32,'rep'=4] {'fsdp','rep'}, use_global_device_ids=true, to_apply=%region_1.2 | all-reduce | flops 1 | bytes 8 | tf_op jit(solution)/shard_map/pmax | solution.py:58
  (2 shorter events, 0.0 us)
Async XLA Ops:
  30.7 12.0 %copy-start = (s32[128,2]{0,1:T(2,128)S(1)}, s32[128,2]{0,1:T(2,128)}, u32[]{:S(2)}) copy-start(s32[128,2]{0,1:T(2,128)} %param.3) | copy-start | bytes 3076
  30.7 116.9 %all-to-all-start = ((bf16[1,1,128,128,256]{4,2,1,0,3:T(8,128)(2,1)}), bf16[1,1,128,128,256]{4,2,1,0,3:T(8,128)(2,1)}, u32[]{:S(2)}, u32[]{:S(2)}) async-start(bf16[1,1,128,128,256]{4,2,1,0,3:T(8,128)(2,1)} %copy.7), calls=%async_computation | async-start | bytes 16777216 | tf_op jit(solution)/shard_map/all_to_all | solution.py:47
where the time goes:
time: 244 us
  waiting for transfers between devices  105 us (43%)
  blocking collectives  66.8 us (27%)
  local copies, waits for them, and re-layouts  32.5 us (13%)
  matrix products  27 us (11%)
  starting transfers between devices  12 us (5%)
    all_to_all x1, waiting for transfers between devices, on_device(): lax.all_to_all(packed, ('fsdp', 'rep'), split_axis=3, concat_axis=0, tile...  105 us
    pmax x1, blocking collectives, on_device(): overall_peak = lax.pmax(local_peak, ('fsdp', 'rep'))  66.8 us
    dot_general x1, matrix products, on_device(): jnp.einsum('pa,aic->pic', outer_table, received.reshape(OUTER, INNER, rec...  17.6 us
    all_to_all x1, starting transfers between devices, on_device(): lax.all_to_all(packed, ('fsdp', 'rep'), split_axis=3, concat_axis=0, tile...  12 us
    reshape x1, local copies, waits for them, and re-layouts, on_device(): packed = moving.reshape(1, outer_local, INNER, devices, cols_dev)  11.5 us
    convert_element_type x1, local copies, waits for them, and re-layouts, on_device(): (rotated * factor).astype(jnp.bfloat16).reshape(OUTER * INNER, cols_dev)  11.5 us
    dot_general x1, matrix products, on_device(): jnp.einsum('ij,ajc->aic', inner_table, source, preferred_element_type=jnp...  9.43 us
    unnamed x4, local copies, waits for them, and re-layouts  9.1 us
  transfers between devices with their start and end apart: 1, of which 1 were waited for; matrix products, arithmetic and copies ran while one was open for 0% of the time, Pallas kernels for 0%

commit v1 on v0

v1 whole, which is shorter than its diff:
```python
import functools

import jax
import jax.numpy as jnp
from jax import lax
from jax.experimental import pallas as pl
from jax.experimental.pallas import tpu as pltpu
from jax.sharding import PartitionSpec as P

INNER = 128
OUTER = 128
HIGH = 8
LOW = 16

low_power = -10
high_power = -5

VMEM_BYTES = 48 * 1024 * 1024


def hadamard(length):
    indices = lax.iota(jnp.int32, length)
    anded = jnp.bitwise_and(indices[:, None], indices[None, :])
    parity = jnp.zeros((length, length), jnp.int32)
    for bit_place in range(length.bit_length()):
        parity = parity + anded // 2**bit_place % 2
    return (1 - 2 * (parity % 2)).astype(jnp.bfloat16)


def block_factor(exponents):
    factor = jnp.zeros(exponents.shape, jnp.float32)
    for exponent in range(low_power, high_power + 1):
        factor = jnp.where(exponents == exponent, jnp.float32(2.0 ** (-exponent)), factor)
    return factor


def butterfly(parts):
    parts = list(parts)
    step = 1
    while step < len(parts):
        for start in range(0, len(parts), 2 * step):
            for at in range(start, start + step):
                first, second = parts[at], parts[at + step]
                parts[at], parts[at + step] = first + second, first - second
        step *= 2
    return parts


def before_kernel(weights_ref, out_ref):
    blocks, _, cols = out_ref.shape
    for block in range(blocks):
        lanes = slice(block * cols, (block + 1) * cols)
        rows = [weights_ref[LOW * k : LOW * (k + 1), lanes].astype(jnp.float32) for k in range(HIGH)]
        for k, row in enumerate(butterfly(rows)):
            out_ref[block, LOW * k : LOW * (k + 1), :] = row.astype(jnp.bfloat16)


def before(weights, devices, blocks=16):
    rows, total = weights.shape
    cols = total // devices
    return pl.pallas_call(
        before_kernel,
        out_shape=jax.ShapeDtypeStruct((devices, rows, cols), jnp.bfloat16),
        grid=(devices // blocks,),
        in_specs=[pl.BlockSpec((rows, blocks * cols), lambda n: (0, n))],
        out_specs=pl.BlockSpec((blocks, rows, cols), lambda n: (n, 0, 0)),
        compiler_params=pltpu.CompilerParams(vmem_limit_bytes=VMEM_BYTES),
        cost_estimate=pl.CostEstimate(flops=3 * rows * total, bytes_accessed=4 * rows * total, transcendentals=0),
    )(weights)


def after_kernel(table_ref, factor_ref, received_ref, out_ref, peak_ref, middle_ref):
    cols = received_ref.shape[-1]
    table = table_ref[...]
    for h in range(HIGH):
        block = received_ref[LOW * h : LOW * (h + 1)].reshape(LOW * LOW, cols)
        middle_ref[h] = jnp.dot(table, block, preferred_element_type=jnp.float32)
    largest = jnp.zeros((LOW, cols), jnp.float32)
    for low in range(LOW):
        rows = [middle_ref[h, LOW * low : LOW * (low + 1), :] for h in range(HIGH)]
        for h, row in enumerate(butterfly(rows)):
            p = h * LOW + low
            row = row * factor_ref[p : p + 1, :]
            largest = jnp.maximum(largest, jnp.abs(row))
            out_ref[p] = row.astype(jnp.bfloat16)

    @pl.when(pl.program_id(0) == 0)
    def _():
        peak_ref[...] = jnp.zeros_like(peak_ref)

    peak_ref[...] = jnp.maximum(peak_ref[...], largest)


def after(table, factor, received):
    outer, inner, cols = received.shape
    return pl.pallas_call(
        after_kernel,
        out_shape=(
            jax.ShapeDtypeStruct((outer, inner, cols), jnp.bfloat16),
            jax.ShapeDtypeStruct((LOW, cols), jnp.float32),
        ),
        grid=(inner // LOW,),
        in_specs=[
            pl.BlockSpec(table.shape, lambda n: (0, 0)),
            pl.BlockSpec(factor.shape, lambda n: (0, 0)),
            pl.BlockSpec((outer, LOW, cols), lambda n: (0, n, 0)),
        ],
        out_specs=(
            pl.BlockSpec((outer, LOW, cols), lambda n: (0, n, 0)),
            pl.BlockSpec((LOW, cols), lambda n: (0, 0)),
        ),
        scratch_shapes=[pltpu.VMEM((HIGH, LOW * LOW, cols), jnp.float32)],
        compiler_params=pltpu.CompilerParams(vmem_limit_bytes=VMEM_BYTES),
        cost_estimate=pl.CostEstimate(
            flops=2 * outer * inner * cols * LOW * LOW, bytes_accessed=4 * outer * inner * cols, transcendentals=0
        ),
    )(table, factor, received)


def on_device(weights, exponents):
    axes = ("fsdp", "rep")
    devices = lax.axis_size("fsdp") * lax.axis_size("rep")
    cols = weights.shape[1] // devices
    table = hadamard(LOW * LOW)
    factor = jnp.repeat(block_factor(exponents) * jnp.float32(1.0 / INNER), INNER, axis=1)
    packed = before(weights, devices)
    received = lax.all_to_all(packed, axes, split_axis=0, concat_axis=0, tiled=True)
    quantized, peaks = after(table, factor, received)
    peak = jnp.max(peaks).astype(jnp.bfloat16).astype(jnp.float32)
    shared = lax.all_to_all(jnp.full((devices, 1, 128), peak), axes, split_axis=0, concat_axis=0, tiled=True)
    return (quantized.reshape(OUTER * INNER, cols), jnp.max(shared))


def solution(mesh):
    return jax.shard_map(
        on_device,
        mesh=mesh,
        in_specs=(P(("fsdp", "rep"), None), P(None, ("fsdp", "rep"))),
        out_specs=(P(None, ("fsdp", "rep")), P()),
        check_vma=False,
    )
```

time: 244 us -> 161 us (0.66)
  blocking collectives: 66.8 us -> 20.2 us
  local copies, waits for them, and re-layouts: 32.5 us -> 1 us
  matrix products: 27 us -> 0 us
  Pallas kernels: 0 us -> 20.8 us
  other arithmetic: 0.01 us -> 2.54 us
    pmax x1 -> x0, blocking collectives: 66.8 us -> none  [on_device(): overall_peak = lax.pmax(local_peak, ('fsdp', 'rep'))]
    dot_general x2 -> x0, matrix products: 27 us -> none  [the longest x1 17.6 us: on_device(): jnp.einsum('pa,aic->pic', outer_table, received.reshape(OUTER, INNER, rec...]
    pallas_call x0 -> x2, Pallas kernels: none -> 20.8 us  [the longest x1 11.1 us: after(): pl.pallas_call(after_kernel, out_shape=(jax.ShapeDtypeStruct((outer, inne...]
    all_to_all x0 -> x1, blocking collectives: none -> 20.2 us  [on_device(): lax.all_to_all(jnp.full((devices, 1, 128), peak), axes, split_axis=0, con...]
    convert_element_type x1 -> x0, local copies, waits for them, and re-layouts: 11.5 us -> none  [on_device(): (rotated * factor).astype(jnp.bfloat16).reshape(OUTER * INNER, cols_dev)]
    reshape x1 -> x0, local copies, waits for them, and re-layouts: 11.5 us -> none  [on_device(): packed = moving.reshape(1, outer_local, INNER, devices, cols_dev)]
    unnamed x4 -> x3, local copies, waits for them, and re-layouts: 9.1 us -> 0.02 us
  transfers between devices with their start and end apart: 1 -> 1, of which waited for: 1 -> 1; matrix products, arithmetic and copies ran while one was open for 0% -> 1% of each run, Pallas kernels for 0% -> 0%
where the time goes in v1:
time: 161 us
  waiting for transfers between devices  103 us (64%)
  Pallas kernels  20.8 us (13%)
  blocking collectives  20.2 us (13%)
  starting transfers between devices  12 us (7%)
  other arithmetic  2.54 us (2%)
    all_to_all x1, waiting for transfers between devices, on_device(): lax.all_to_all(packed, axes, split_axis=0, concat_axis=0, tiled=True)  103 us
    all_to_all x1, blocking collectives, on_device(): lax.all_to_all(jnp.full((devices, 1, 128), peak), axes, split_axis=0, con...  20.2 us
    all_to_all x1, starting transfers between devices, on_device(): lax.all_to_all(packed, axes, split_axis=0, concat_axis=0, tiled=True)  12 us
    pallas_call x1, Pallas kernels, after(): pl.pallas_call(after_kernel, out_shape=(jax.ShapeDtypeStruct((outer, inne...  11.1 us
    pallas_call x1, Pallas kernels, before(): pl.pallas_call(before_kernel, out_shape=jax.ShapeDtypeStruct((devices, ro...  9.79 us
  transfers between devices with their start and end apart: 1, of which 1 were waited for; matrix products, arithmetic and copies ran while one was open for 1% of the time, Pallas kernels for 0%

profile of v1, /device:TPU:1, one launch (start us, length us, event | category | flops | bytes accessed | tf_op | source)
XLA Modules:
  0.0 160.5 jit_solution(4357377720673771392)
XLA Ops:
  0.6 9.8 %shard_map.41 = bf16[128,128,256]{2,1,0:T(8,128)(2,1)} custom-call(bf16[128,32768]{1,0:T(8,128)(2,1)} %weights_ref.1), custom_call_target="tpu_custom_call" | custom-call | flops 12582912 | bytes 16777216 | tf_op jit(solution)/shard_map/pallas_call | solution.py:61
  10.4 0.0 copy-start
  10.4 12.0 %all-to-all-start = ((bf16[128,128,256]{2,1,0:T(8,128)(2,1)}), bf16[128,128,256]{2,1,0:T(8,128)(2,1)}, u32[]{:S(2)}, u32[]{:S(2)}) async-start(bf16[128,128,256]{2,1,0:T(8,128)(2,1)} %shard_map.41), calls=%async_computation | async-start | bytes 16777216 | tf_op jit(solution)/shard_map/all_to_all | solution.py:127
  22.4 0.0 copy-done
  22.4 0.1 copy.6
  22.5 0.2 broadcast_in_dim.37
  22.7 1.3 fusion.26.table_ref
  24.1 103.4 %all-to-all-done.received_ref = bf16[128,128,256]{2,1,0:T(8,128)(2,1)} async-done(((bf16[128,128,256]{2,1,0:T(8,128)(2,1)}), bf16[128,128,256]{2,1,0:T(8,128)(2,1)}, u32[]{:S(2)}, u32[]{:S(2)}) %all-to-all-start) | async-done | bytes 8388640 | tf_op jit(solution)/shard_map/all_to_all | solution.py:127
  127.4 11.1 %shard_map.42 = (bf16[128,128,256]{2,1,0:T(8,128)(2,1)}, f32[16,256]{1,0:T(8,128)S(1)}) custom-call(bf16[256,256]{1,0:T(8,128)(2,1)S(1)} %fusion.26.table_ref, f32[128,256]{1,0:T(8,128)S(1)} %bitcast.6, bf16[128,128,256]{2,1,0:T(8,128)(2,1)} %all-to-all-done.received_ref), custom_call_target="tpu_custom_call" | custom-call | flops 2147483648 | bytes 16777216 | tf_op jit(solution)/shard_map/pallas_call | solution.py:96
  138.5 0.6 reduce_max.18
  139.1 0.7 broadcast_in_dim.38
  139.8 20.2 %all_to_all.10 = f32[128,1,128]{2,1,0:T(1,128)S(1)} all-to-all(f32[128,1,128]{2,1,0:T(1,128)S(1)} %broadcast_in_dim.38), channel_id=1, replica_groups=mesh['fsdp'=32,'rep'=4] {'fsdp','rep'}, dimensions={0} | all-to-all | bytes 131072 | tf_op jit(solution)/shard_map/all_to_all | solution.py:130
  159.9 0.6 reduce_max.19
  (2 shorter events, 0.0 us)
Async XLA Ops:
  10.4 12.0 %copy-start = (s32[128,2]{0,1:T(2,128)S(1)}, s32[128,2]{0,1:T(2,128)}, u32[]{:S(2)}) copy-start(s32[128,2]{0,1:T(2,128)} %param.3) | copy-start | bytes 3076
  10.4 117.0 %all-to-all-start = ((bf16[128,128,256]{2,1,0:T(8,128)(2,1)}), bf16[128,128,256]{2,1,0:T(8,128)(2,1)}, u32[]{:S(2)}, u32[]{:S(2)}) async-start(bf16[128,128,256]{2,1,0:T(8,128)(2,1)} %shard_map.41), calls=%async_computation | async-start | bytes 16777216 | tf_op jit(solution)/shard_map/all_to_all | solution.py:127

commit v2 on v1

v2 whole, which is shorter than its diff:
```python
import functools

import jax
import jax.numpy as jnp
from jax import lax
from jax.experimental import pallas as pl
from jax.experimental.pallas import tpu as pltpu
from jax.sharding import PartitionSpec as P

INNER = 128
OUTER = 128
HIGH = 8
LOW = 16

low_power = -10
high_power = -5

PIECES = 8

VMEM_BYTES = 20 * 1024 * 1024


def sylvester(length):
    bits = lax.broadcasted_iota(jnp.int32, (length, length), 0) & lax.broadcasted_iota(jnp.int32, (length, length), 1)
    for shift in (4, 2, 1):
        bits = bits ^ (bits >> shift)
    return (1 - 2 * (bits & 1)).astype(jnp.float32).astype(jnp.bfloat16)


def block_factor(exponents):
    factor = jnp.zeros(exponents.shape, jnp.float32)
    for exponent in range(low_power, high_power + 1):
        factor = jnp.where(exponents == exponent, jnp.float32(2.0 ** (-exponent)), factor)
    return factor


def butterfly(parts):
    parts = list(parts)
    step = 1
    while step < len(parts):
        for start in range(0, len(parts), 2 * step):
            for at in range(start, start + step):
                first, second = parts[at], parts[at + step]
                parts[at], parts[at + step] = first + second, first - second
        step *= 2
    return parts


def before_kernel(weights_ref, out_ref, held_ref, arrived):
    devices, _, cols = out_ref.shape
    pieces = arrived.shape[0]
    blocks = devices // pieces

    def fetch(piece):
        lanes = pl.ds(pl.multiple_of(piece * blocks * cols, blocks * cols), blocks * cols)
        return pltpu.make_async_copy(weights_ref.at[:, lanes], held_ref.at[:, lanes], arrived.at[piece])

    for piece in range(pieces):
        fetch(piece).start()

    def work(piece, carry):
        fetch(piece).wait()
        for at in range(blocks):
            block = piece * blocks + at
            lanes = pl.ds(pl.multiple_of(block * cols, cols), cols)
            rows = [held_ref[LOW * k : LOW * (k + 1), lanes].astype(jnp.float32) for k in range(HIGH)]
            for k, row in enumerate(butterfly(rows)):
                out_ref[block, LOW * k : LOW * (k + 1), :] = row.astype(jnp.bfloat16)
        return carry

    lax.fori_loop(0, pieces, work, 0)


def before(weights, devices):
    rows, total = weights.shape
    return pl.pallas_call(
        before_kernel,
        out_shape=pltpu.VMEM((devices, rows, total // devices), jnp.bfloat16),
        in_specs=[pl.BlockSpec(memory_space=pl.ANY)],
        out_specs=pl.BlockSpec(memory_space=pltpu.VMEM),
        scratch_shapes=[pltpu.VMEM(weights.shape, jnp.bfloat16), pltpu.SemaphoreType.DMA((PIECES,))],
        compiler_params=pltpu.CompilerParams(vmem_limit_bytes=VMEM_BYTES),
    )(pltpu.with_memory_space_constraint(weights, pltpu.HBM))


def after_kernel(exponents_ref, received_ref, out_ref, peak_ref, factor_ref, stage_ref, even_ref, odd_ref, written):
    cols = received_ref.shape[-1]
    groups = INNER // LOW
    table = sylvester(LOW * LOW)
    scale = block_factor(exponents_ref[...]) * jnp.float32(1.0 / INNER)
    for half in range(scale.shape[0]):
        spread = jnp.broadcast_to(scale[half : half + 1, :], (INNER, OUTER))
        factor_ref[:, half * INNER : (half + 1) * INNER] = jnp.transpose(spread)

    def rows_of(group):
        return pl.ds(pl.multiple_of(group * LOW, LOW), LOW)

    def write(group):
        return pltpu.make_async_copy(stage_ref.at[group], out_ref.at[:, rows_of(group), :], written.at[group])

    def multiply(group, middle_ref):
        for h in range(HIGH):
            block = received_ref[LOW * h : LOW * (h + 1), rows_of(group), :].reshape(LOW * LOW, cols)
            middle_ref[h] = jnp.dot(table, block, preferred_element_type=jnp.float32)

    def finish(group, middle_ref, largest):
        for low in range(LOW):
            parts = [middle_ref[h, LOW * low : LOW * (low + 1), :] for h in range(HIGH)]
            for h, part in enumerate(butterfly(parts)):
                p = h * LOW + low
                part = (part * factor_ref[p : p + 1, :]).astype(jnp.bfloat16)
                largest = jnp.maximum(largest, jnp.abs(part))
                stage_ref[group, p] = part
        write(group).start()
        return largest

    multiply(0, even_ref)

    def pair(at, largest):
        multiply(2 * at + 1, odd_ref)
        largest = finish(2 * at, even_ref, largest)
        multiply(lax.rem(2 * at + 2, groups), even_ref)
        return finish(2 * at + 1, odd_ref, largest)

    largest = lax.fori_loop(0, groups // 2, pair, jnp.zeros((LOW, cols), jnp.bfloat16))
    peak = jnp.max(largest.astype(jnp.float32), axis=(0, 1), keepdims=True)
    peak_ref[...] = jnp.broadcast_to(peak.reshape(1, 1, 1), peak_ref.shape)
    for group in range(groups):
        write(group).wait()


def after(exponents, received, devices):
    outer, inner, cols = received.shape
    groups = inner // LOW
    return pl.pallas_call(
        after_kernel,
        out_shape=(
            jax.ShapeDtypeStruct((outer, inner, cols), jnp.bfloat16),
            pltpu.VMEM((devices, 1, 128), jnp.float32),
        ),
        in_specs=[pl.BlockSpec(memory_space=pltpu.VMEM)] * 2,
        out_specs=(pl.BlockSpec(memory_space=pl.ANY), pl.BlockSpec(memory_space=pltpu.VMEM)),
        scratch_shapes=[
            pltpu.VMEM((outer, cols), jnp.float32),
            pltpu.VMEM((groups, outer, LOW, cols), jnp.bfloat16),
            pltpu.VMEM((HIGH, LOW * LOW, cols), jnp.float32),
            pltpu.VMEM((HIGH, LOW * LOW, cols), jnp.float32),
            pltpu.SemaphoreType.DMA((groups,)),
        ],
        compiler_params=pltpu.CompilerParams(vmem_limit_bytes=VMEM_BYTES),
    )(exponents, pltpu.with_memory_space_constraint(received, pltpu.VMEM))


def on_device(weights, exponents):
    axes = ("fsdp", "rep")
    devices = lax.axis_size("fsdp") * lax.axis_size("rep")
    cols = weights.shape[1] // devices
    packed = before(weights, devices)
    received = lax.all_to_all(packed, axes, split_axis=0, concat_axis=0, tiled=True)
    quantized, peaks = after(exponents.T, received, devices)
    shared = lax.all_to_all(peaks, axes, split_axis=0, concat_axis=0, tiled=True)
    return (quantized.reshape(OUTER * INNER, cols), jnp.max(shared))


def solution(mesh):
    return jax.shard_map(
        on_device,
        mesh=mesh,
        in_specs=(P(("fsdp", "rep"), None), P(None, ("fsdp", "rep"))),
        out_specs=(P(None, ("fsdp", "rep")), P()),
        check_vma=False,
    )
```

time: 161 us -> 144 us (0.89)
  blocking collectives: 20.2 us -> 131 us
  waiting for transfers between devices: 103 us -> 0 us
  starting transfers between devices: 12 us -> 0 us
  Pallas kernels: 20.8 us -> 10.8 us
  other arithmetic: 2.54 us -> 0.73 us
    all_to_all x1 -> x2, blocking collectives: 20.2 us -> 131 us  [the longest x1 109 us: on_device(): lax.all_to_all(packed, axes, split_axis=0, concat_axis=0, tiled=True)]
    all_to_all x1 -> x0, waiting for transfers between devices: 103 us -> none  [on_device(): lax.all_to_all(packed, axes, split_axis=0, concat_axis=0, tiled=True)]
    all_to_all x1 -> x0, starting transfers between devices: 12 us -> none  [on_device(): lax.all_to_all(packed, axes, split_axis=0, concat_axis=0, tiled=True)]
    pallas_call x1, Pallas kernels: 9.79 us -> 3.81 us  [before(): pl.pallas_call(before_kernel, out_shape=pltpu.VMEM((devices, rows, total...]
    pallas_call x1, Pallas kernels: 11.1 us -> 7.02 us  [after(): pl.pallas_call(after_kernel, out_shape=(jax.ShapeDtypeStruct((outer, inne...]
  transfers between devices with their start and end apart: 1 -> 0, of which waited for: 1 -> 0; matrix products, arithmetic and copies ran while one was open for 1% -> 0% of each run, Pallas kernels for 0% -> 0%
where the time goes in v2:
time: 144 us
  blocking collectives  131 us (91%)
  Pallas kernels  10.8 us (8%)
    all_to_all x1, blocking collectives, on_device(): lax.all_to_all(packed, axes, split_axis=0, concat_axis=0, tiled=True)  109 us
    all_to_all x1, blocking collectives, on_device(): lax.all_to_all(peaks, axes, split_axis=0, concat_axis=0, tiled=True)  22.6 us
    pallas_call x1, Pallas kernels, after(): pl.pallas_call(after_kernel, out_shape=(jax.ShapeDtypeStruct((outer, inne...  7.02 us
    pallas_call x1, Pallas kernels, before(): pl.pallas_call(before_kernel, out_shape=pltpu.VMEM((devices, rows, total...  3.81 us

profile of v2, /device:TPU:1, one launch (start us, length us, event | category | flops | bytes accessed | tf_op | source)
XLA Modules:
  0.0 143.5 jit_solution(13677949786266589092)
XLA Ops:
  0.6 3.8 %shard_map.41 = bf16[128,128,256]{2,1,0:T(8,128)(2,1)S(1)} custom-call(bf16[128,32768]{1,0:T(8,128)(2,1)} %weights_ref.1), custom_call_target="tpu_custom_call" | custom-call | tf_op jit(solution)/shard_map/pallas_call | solution.py:76
  4.4 0.0 copy-start
  4.5 108.7 %all_to_all.10.received_ref = bf16[128,128,256]{2,1,0:T(8,128)(2,1)S(1)} all-to-all(bf16[128,128,256]{2,1,0:T(8,128)(2,1)S(1)} %shard_map.41), channel_id=1, replica_groups=mesh['fsdp'=32,'rep'=4] {'fsdp','rep'}, dimensions={0} | all-to-all | bytes 16777216 | tf_op jit(solution)/shard_map/all_to_all | solution.py:159
  113.1 0.0 copy-done
  113.1 7.0 %shard_map.42 = (bf16[128,128,256]{2,1,0:T(8,128)(2,1)}, f32[128,1,128]{2,1,0:T(1,128)S(1)}) custom-call(s32[2,128]{1,0:T(2,128)S(1)} %bitcast.2, bf16[128,128,256]{2,1,0:T(8,128)(2,1)S(1)} %all_to_all.10.received_ref), custom_call_target="tpu_custom_call" | custom-call | tf_op jit(solution)/shard_map/pallas_call | solution.py:135
  120.2 22.6 %all_to_all.11 = f32[128,1,128]{2,1,0:T(1,128)S(1)} all-to-all(f32[128,1,128]{2,1,0:T(1,128)S(1)} %get-tuple-element.5), channel_id=1, replica_groups=mesh['fsdp'=32,'rep'=4] {'fsdp','rep'}, dimensions={0} | all-to-all | bytes 131072 | tf_op jit(solution)/shard_map/all_to_all | solution.py:161
  142.8 0.7 reduce_max.9
Async XLA Ops:
  4.4 108.7 %copy-start = (s32[128,2]{0,1:T(2,128)S(1)}, s32[128,2]{0,1:T(2,128)}, u32[]{:S(2)}) copy-start(s32[128,2]{0,1:T(2,128)} %param.3) | copy-start | bytes 3076

commit v3 on v2

--- a/solution.py
+++ b/solution.py
@@ -16,6 +16,7 @@
 high_power = -5
 
 PIECES = 8
+EXCHANGE_BITS = (5, 4, 0, 1, 6, 3, 2)
 
 VMEM_BYTES = 20 * 1024 * 1024
 
@@ -25,6 +26,16 @@
     for shift in (4, 2, 1):
         bits = bits ^ (bits >> shift)
     return (1 - 2 * (bits & 1)).astype(jnp.float32).astype(jnp.bfloat16)
+
+
+def device_at(position):
+    last = len(EXCHANGE_BITS) - 1
+    return sum(((position >> (last - at)) & 1) << bit for at, bit in enumerate(EXCHANGE_BITS))
+
+
+def position_of(device):
+    last = len(EXCHANGE_BITS) - 1
+    return sum(((device >> bit) & 1) << (last - at) for at, bit in enumerate(EXCHANGE_BITS))
 
 
 def block_factor(exponents):
@@ -60,9 +71,10 @@
 
     def work(piece, carry):
         fetch(piece).wait()
+        first = position_of(piece * blocks)
         for at in range(blocks):
-            block = piece * blocks + at
-            lanes = pl.ds(pl.multiple_of(block * cols, cols), cols)
+            block = first + position_of(at)
+            lanes = pl.ds(pl.multiple_of((piece * blocks + at) * cols, cols), cols)
             rows = [held_ref[LOW * k : LOW * (k + 1), lanes].astype(jnp.float32) for k in range(HIGH)]
             for k, row in enumerate(butterfly(rows)):
                 out_ref[block, LOW * k : LOW * (k + 1), :] = row.astype(jnp.bfloat16)
@@ -98,29 +110,29 @@
     def write(group):
         return pltpu.make_async_copy(stage_ref.at[group], out_ref.at[:, rows_of(group), :], written.at[group])
 
-    def multiply(group, middle_ref):
-        for h in range(HIGH):
-            block = received_ref[LOW * h : LOW * (h + 1), rows_of(group), :].reshape(LOW * LOW, cols)
-            middle_ref[h] = jnp.dot(table, block, preferred_element_type=jnp.float32)
+    def multiply(group, h, middle_ref):
+        block = received_ref[LOW * h : LOW * (h + 1), rows_of(group), :].reshape(LOW * LOW, cols)
+        middle_ref[h] = jnp.dot(table, block, preferred_element_type=jnp.float32)
 
-    def finish(group, middle_ref, largest):
+    def step(group, middle_ref, following, following_ref, largest):
         for low in range(LOW):
+            if low % 2 == 0:
+                multiply(following, low // 2, following_ref)
             parts = [middle_ref[h, LOW * low : LOW * (low + 1), :] for h in range(HIGH)]
             for h, part in enumerate(butterfly(parts)):
-                p = h * LOW + low
+                p = device_at(h * LOW + low)
                 part = (part * factor_ref[p : p + 1, :]).astype(jnp.bfloat16)
                 largest = jnp.maximum(largest, jnp.abs(part))
                 stage_ref[group, p] = part
         write(group).start()
         return largest
 
-    multiply(0, even_ref)
+    for h in range(HIGH):
+        multiply(0, h, even_ref)
 
     def pair(at, largest):
-        multiply(2 * at + 1, odd_ref)
-        largest = finish(2 * at, even_ref, largest)
-        multiply(lax.rem(2 * at + 2, groups), even_ref)
-        return finish(2 * at + 1, odd_ref, largest)
+        largest = step(2 * at, even_ref, 2 * at + 1, odd_ref, largest)
+        return step(2 * at + 1, odd_ref, lax.rem(2 * at + 2, groups), even_ref, largest)
 
     largest = lax.fori_loop(0, groups // 2, pair, jnp.zeros((LOW, cols), jnp.bfloat16))
     peak = jnp.max(largest.astype(jnp.float32), axis=(0, 1), keepdims=True)
@@ -156,9 +168,13 @@
     devices = lax.axis_size("fsdp") * lax.axis_size("rep")
     cols = weights.shape[1] // devices
     packed = before(weights, devices)
-    received = lax.all_to_all(packed, axes, split_axis=0, concat_axis=0, tiled=True)
+    order = [[device_at(position) for position in range(devices)]]
+    exchange = functools.partial(
+        lax.all_to_all, axis_name=axes, split_axis=0, concat_axis=0, axis_index_groups=order, tiled=True
+    )
+    received = exchange(packed)
     quantized, peaks = after(exponents.T, received, devices)
-    shared = lax.all_to_all(peaks, axes, split_axis=0, concat_axis=0, tiled=True)
+    shared = exchange(peaks)
     return (quantized.reshape(OUTER * INNER, cols), jnp.max(shared))
 
 

time: 144 us -> 135 us (0.938)
  blocking collectives: 131 us -> 123 us
    all_to_all x2, blocking collectives: 131 us -> 123 us  [the longest x1 108 us: on_device(): received = exchange(packed)]
where the time goes in v3:
time: 135 us
  blocking collectives  123 us (91%)
  Pallas kernels  10.8 us (8%)
    all_to_all x1, blocking collectives, on_device(): received = exchange(packed)  108 us
    all_to_all x1, blocking collectives, on_device(): shared = exchange(peaks)  14.4 us
    pallas_call x1, Pallas kernels, after(): pl.pallas_call(after_kernel, out_shape=(jax.ShapeDtypeStruct((outer, inne...  6.98 us
    pallas_call x1, Pallas kernels, before(): pl.pallas_call(before_kernel, out_shape=pltpu.VMEM((devices, rows, total...  3.83 us

profile of v3, /device:TPU:1, one launch (start us, length us, event | category | flops | bytes accessed | tf_op | source)
XLA Modules:
  0.0 134.8 jit_solution(13100653198569669492)
XLA Ops:
  0.6 3.8 %shard_map.41 = bf16[128,128,256]{2,1,0:T(8,128)(2,1)S(1)} custom-call(bf16[128,32768]{1,0:T(8,128)(2,1)} %weights_ref.1), custom_call_target="tpu_custom_call" | custom-call | tf_op jit(solution)/shard_map/pallas_call | solution.py:88
  4.5 0.0 copy-start
  4.5 108.1 %all_to_all.10.received_ref = bf16[128,128,256]{2,1,0:T(8,128)(2,1)S(1)} all-to-all(bf16[128,128,256]{2,1,0:T(8,128)(2,1)S(1)} %shard_map.41), channel_id=1, replica_groups={{0,4,8,12,64,68,72,76,2,6,10,14,66,70,74,78,1,5,9,13,65,69,73,77,3,7,11..., dimensions={0} | all-to-all | bytes 16777216 | tf_op jit(solution)/shard_map/all_to_all | solution.py:175
  112.6 0.0 copy-done
  112.6 7.0 %shard_map.42 = (bf16[128,128,256]{2,1,0:T(8,128)(2,1)}, f32[128,1,128]{2,1,0:T(1,128)S(1)}) custom-call(s32[2,128]{1,0:T(2,128)S(1)} %bitcast.2, bf16[128,128,256]{2,1,0:T(8,128)(2,1)S(1)} %all_to_all.10.received_ref), custom_call_target="tpu_custom_call" | custom-call | tf_op jit(solution)/shard_map/pallas_call | solution.py:147
  119.6 14.4 %all_to_all.11 = f32[128,1,128]{2,1,0:T(1,128)S(1)} all-to-all(f32[128,1,128]{2,1,0:T(1,128)S(1)} %get-tuple-element.5), channel_id=1, replica_groups={{0,4,8,12,64,68,72,76,2,6,10,14,66,70,74,78,1,5,9,13,65,69,73,77,3,7,11..., dimensions={0} | all-to-all | bytes 131072 | tf_op jit(solution)/shard_map/all_to_all | solution.py:177
  134.0 0.7 reduce_max.9
Async XLA Ops:
  4.5 108.1 %copy-start = (s32[128,2]{0,1:T(2,128)S(1)}, s32[128,2]{0,1:T(2,128)}, u32[]{:S(2)}) copy-start(s32[128,2]{0,1:T(2,128)} %param.3) | copy-start | bytes 3076

commit v4 on v3

--- a/solution.py
+++ b/solution.py
@@ -105,7 +105,7 @@
         factor_ref[:, half * INNER : (half + 1) * INNER] = jnp.transpose(spread)
 
     def rows_of(group):
-        return pl.ds(pl.multiple_of(group * LOW, LOW), LOW)
+        return slice(group * LOW, (group + 1) * LOW)
 
     def write(group):
         return pltpu.make_async_copy(stage_ref.at[group], out_ref.at[:, rows_of(group), :], written.at[group])
@@ -116,7 +116,7 @@
 
     def step(group, middle_ref, following, following_ref, largest):
         for low in range(LOW):
-            if low % 2 == 0:
+            if low % 2 == 0 and following < groups:
                 multiply(following, low // 2, following_ref)
             parts = [middle_ref[h, LOW * low : LOW * (low + 1), :] for h in range(HIGH)]
             for h, part in enumerate(butterfly(parts)):
@@ -130,11 +130,10 @@
     for h in range(HIGH):
         multiply(0, h, even_ref)
 
-    def pair(at, largest):
-        largest = step(2 * at, even_ref, 2 * at + 1, odd_ref, largest)
-        return step(2 * at + 1, odd_ref, lax.rem(2 * at + 2, groups), even_ref, largest)
-
-    largest = lax.fori_loop(0, groups // 2, pair, jnp.zeros((LOW, cols), jnp.bfloat16))
+    largest = jnp.zeros((LOW, cols), jnp.bfloat16)
+    refs = (even_ref, odd_ref)
+    for group in range(groups):
+        largest = step(group, refs[group % 2], group + 1, refs[(group + 1) % 2], largest)
     peak = jnp.max(largest.astype(jnp.float32), axis=(0, 1), keepdims=True)
     peak_ref[...] = jnp.broadcast_to(peak.reshape(1, 1, 1), peak_ref.shape)
     for group in range(groups):

time: 135 us -> 134 us (level)
  no operation moved by 1% of the time
where the time goes in v4:
time: 134 us
  blocking collectives  123 us (92%)
  Pallas kernels  9.8 us (7%)
    all_to_all x1, blocking collectives, on_device(): received = exchange(packed)  108 us
    all_to_all x1, blocking collectives, on_device(): shared = exchange(peaks)  14.4 us
    pallas_call x1, Pallas kernels, after(): pl.pallas_call(after_kernel, out_shape=(jax.ShapeDtypeStruct((outer, inne...  5.97 us
    pallas_call x1, Pallas kernels, before(): pl.pallas_call(before_kernel, out_shape=pltpu.VMEM((devices, rows, total...  3.83 us

profile of v4, /device:TPU:1, one launch (start us, length us, event | category | flops | bytes accessed | tf_op | source)
XLA Modules:
  0.0 133.8 jit_solution(18307768741482056449)
XLA Ops:
  0.6 3.8 %shard_map.41 = bf16[128,128,256]{2,1,0:T(8,128)(2,1)S(1)} custom-call(bf16[128,32768]{1,0:T(8,128)(2,1)} %weights_ref.1), custom_call_target="tpu_custom_call" | custom-call | tf_op jit(solution)/shard_map/pallas_call | solution.py:88
  4.5 0.0 copy-start
  4.5 108.1 %all_to_all.10.received_ref = bf16[128,128,256]{2,1,0:T(8,128)(2,1)S(1)} all-to-all(bf16[128,128,256]{2,1,0:T(8,128)(2,1)S(1)} %shard_map.41), channel_id=1, replica_groups={{0,4,8,12,64,68,72,76,2,6,10,14,66,70,74,78,1,5,9,13,65,69,73,77,3,7,11..., dimensions={0} | all-to-all | bytes 16777216 | tf_op jit(solution)/shard_map/all_to_all | solution.py:174
  112.6 0.0 copy-done
  112.6 6.0 %shard_map.42 = (bf16[128,128,256]{2,1,0:T(8,128)(2,1)}, f32[128,1,128]{2,1,0:T(1,128)S(1)}) custom-call(s32[2,128]{1,0:T(2,128)S(1)} %bitcast.2, bf16[128,128,256]{2,1,0:T(8,128)(2,1)S(1)} %all_to_all.10.received_ref), custom_call_target="tpu_custom_call" | custom-call | tf_op jit(solution)/shard_map/pallas_call | solution.py:146
  118.6 14.4 %all_to_all.11 = f32[128,1,128]{2,1,0:T(1,128)S(1)} all-to-all(f32[128,1,128]{2,1,0:T(1,128)S(1)} %get-tuple-element.5), channel_id=1, replica_groups={{0,4,8,12,64,68,72,76,2,6,10,14,66,70,74,78,1,5,9,13,65,69,73,77,3,7,11..., dimensions={0} | all-to-all | bytes 131072 | tf_op jit(solution)/shard_map/all_to_all | solution.py:176
  133.0 0.7 reduce_max.9
Async XLA Ops:
  4.5 108.1 %copy-start = (s32[128,2]{0,1:T(2,128)S(1)}, s32[128,2]{0,1:T(2,128)}, u32[]{:S(2)}) copy-start(s32[128,2]{0,1:T(2,128)} %param.3) | copy-start | bytes 3076

commit v5 on v4

--- a/solution.py
+++ b/solution.py
@@ -15,7 +15,7 @@
 low_power = -10
 high_power = -5
 
-PIECES = 8
+PIECES = 16
 EXCHANGE_BITS = (5, 4, 0, 1, 6, 3, 2)
 
 VMEM_BYTES = 20 * 1024 * 1024
@@ -110,30 +110,28 @@
     def write(group):
         return pltpu.make_async_copy(stage_ref.at[group], out_ref.at[:, rows_of(group), :], written.at[group])
 
-    def multiply(group, h, middle_ref):
-        block = received_ref[LOW * h : LOW * (h + 1), rows_of(group), :].reshape(LOW * LOW, cols)
-        middle_ref[h] = jnp.dot(table, block, preferred_element_type=jnp.float32)
+    def prepare(group, low, middle_ref):
+        parts = [received_ref[h * LOW + low, rows_of(group), :] for h in range(HIGH)]
+        for h, part in enumerate(butterfly(parts)):
+            middle_ref[h, LOW * low : LOW * (low + 1), :] = part.astype(jnp.bfloat16)
 
-    def step(group, middle_ref, following, following_ref, largest):
-        for low in range(LOW):
-            if low % 2 == 0 and following < groups:
-                multiply(following, low // 2, following_ref)
-            parts = [middle_ref[h, LOW * low : LOW * (low + 1), :] for h in range(HIGH)]
-            for h, part in enumerate(butterfly(parts)):
+    refs = (even_ref, odd_ref)
+    for low in range(LOW):
+        prepare(0, low, even_ref)
+    largest = jnp.zeros((LOW, cols), jnp.bfloat16)
+    for group in range(groups):
+        for h in range(HIGH):
+            product = jnp.dot(table, refs[group % 2][h], preferred_element_type=jnp.float32)
+            if group + 1 < groups:
+                for low in (2 * h, 2 * h + 1):
+                    prepare(group + 1, low, refs[(group + 1) % 2])
+            for low in range(LOW):
                 p = device_at(h * LOW + low)
-                part = (part * factor_ref[p : p + 1, :]).astype(jnp.bfloat16)
+                part = (product[LOW * low : LOW * (low + 1), :] * factor_ref[p : p + 1, :]).astype(jnp.bfloat16)
                 largest = jnp.maximum(largest, jnp.abs(part))
                 stage_ref[group, p] = part
         write(group).start()
-        return largest
 
-    for h in range(HIGH):
-        multiply(0, h, even_ref)
-
-    largest = jnp.zeros((LOW, cols), jnp.bfloat16)
-    refs = (even_ref, odd_ref)
-    for group in range(groups):
-        largest = step(group, refs[group % 2], group + 1, refs[(group + 1) % 2], largest)
     peak = jnp.max(largest.astype(jnp.float32), axis=(0, 1), keepdims=True)
     peak_ref[...] = jnp.broadcast_to(peak.reshape(1, 1, 1), peak_ref.shape)
     for group in range(groups):
@@ -154,8 +152,8 @@
         scratch_shapes=[
             pltpu.VMEM((outer, cols), jnp.float32),
             pltpu.VMEM((groups, outer, LOW, cols), jnp.bfloat16),
-            pltpu.VMEM((HIGH, LOW * LOW, cols), jnp.float32),
-            pltpu.VMEM((HIGH, LOW * LOW, cols), jnp.float32),
+            pltpu.VMEM((HIGH, LOW * LOW, cols), jnp.bfloat16),
+            pltpu.VMEM((HIGH, LOW * LOW, cols), jnp.bfloat16),
             pltpu.SemaphoreType.DMA((groups,)),
         ],
         compiler_params=pltpu.CompilerParams(vmem_limit_bytes=VMEM_BYTES),

time: 134 us -> 133 us (level)
  no operation moved by 1% of the time
where the time goes in v5:
time: 133 us
  blocking collectives  123 us (92%)
  Pallas kernels  8.93 us (7%)
    all_to_all x1, blocking collectives, on_device(): received = exchange(packed)  108 us
    all_to_all x1, blocking collectives, on_device(): shared = exchange(peaks)  14.4 us
    pallas_call x1, Pallas kernels, after(): pl.pallas_call(after_kernel, out_shape=(jax.ShapeDtypeStruct((outer, inne...  5.12 us
    pallas_call x1, Pallas kernels, before(): pl.pallas_call(before_kernel, out_shape=pltpu.VMEM((devices, rows, total...  3.81 us

profile of v5, /device:TPU:1, one launch (start us, length us, event | category | flops | bytes accessed | tf_op | source)
XLA Modules:
  0.0 132.9 jit_solution(12110025345452973709)
XLA Ops:
  0.6 3.8 %shard_map.41 = bf16[128,128,256]{2,1,0:T(8,128)(2,1)S(1)} custom-call(bf16[128,32768]{1,0:T(8,128)(2,1)} %weights_ref.1), custom_call_target="tpu_custom_call" | custom-call | tf_op jit(solution)/shard_map/pallas_call | solution.py:88
  4.4 0.0 copy-start
  4.5 108.1 %all_to_all.10.received_ref = bf16[128,128,256]{2,1,0:T(8,128)(2,1)S(1)} all-to-all(bf16[128,128,256]{2,1,0:T(8,128)(2,1)S(1)} %shard_map.41), channel_id=1, replica_groups={{0,4,8,12,64,68,72,76,2,6,10,14,66,70,74,78,1,5,9,13,65,69,73,77,3,7,11..., dimensions={0} | all-to-all | bytes 16777216 | tf_op jit(solution)/shard_map/all_to_all | solution.py:172
  112.6 0.0 copy-done
  112.6 5.1 %shard_map.42 = (bf16[128,128,256]{2,1,0:T(8,128)(2,1)}, f32[128,1,128]{2,1,0:T(1,128)S(1)}) custom-call(s32[2,128]{1,0:T(2,128)S(1)} %bitcast.2, bf16[128,128,256]{2,1,0:T(8,128)(2,1)S(1)} %all_to_all.10.received_ref), custom_call_target="tpu_custom_call" | custom-call | tf_op jit(solution)/shard_map/pallas_call | solution.py:144
  117.7 14.4 %all_to_all.11 = f32[128,1,128]{2,1,0:T(1,128)S(1)} all-to-all(f32[128,1,128]{2,1,0:T(1,128)S(1)} %get-tuple-element.5), channel_id=1, replica_groups={{0,4,8,12,64,68,72,76,2,6,10,14,66,70,74,78,1,5,9,13,65,69,73,77,3,7,11..., dimensions={0} | all-to-all | bytes 131072 | tf_op jit(solution)/shard_map/all_to_all | solution.py:174
  132.2 0.7 reduce_max.9
Async XLA Ops:
  4.4 108.1 %copy-start = (s32[128,2]{0,1:T(2,128)S(1)}, s32[128,2]{0,1:T(2,128)}, u32[]{:S(2)}) copy-start(s32[128,2]{0,1:T(2,128)} %param.3) | copy-start | bytes 3076

commit v6 on v5

--- a/solution.py
+++ b/solution.py
@@ -16,6 +16,8 @@
 high_power = -5
 
 PIECES = 16
+WIDE = 2
+WRITTEN = 4
 EXCHANGE_BITS = (5, 4, 0, 1, 6, 3, 2)
 
 VMEM_BYTES = 20 * 1024 * 1024
@@ -104,38 +106,45 @@
         spread = jnp.broadcast_to(scale[half : half + 1, :], (INNER, OUTER))
         factor_ref[:, half * INNER : (half + 1) * INNER] = jnp.transpose(spread)
 
-    def rows_of(group):
-        return slice(group * LOW, (group + 1) * LOW)
-
-    def write(group):
-        return pltpu.make_async_copy(stage_ref.at[group], out_ref.at[:, rows_of(group), :], written.at[group])
+    def write(group, first):
+        outer = slice(first * LOW, (first + WRITTEN) * LOW)
+        rows = slice(group * LOW, (group + 1) * LOW)
+        return pltpu.make_async_copy(
+            stage_ref.at[group, outer], out_ref.at[outer, rows, :], written.at[group, first // WRITTEN]
+        )
 
     def prepare(group, low, middle_ref):
-        parts = [received_ref[h * LOW + low, rows_of(group), :] for h in range(HIGH)]
+        rows = slice(group * LOW, (group + 1) * LOW)
+        parts = [received_ref[position_of(h * LOW + low), rows, :] for h in range(HIGH)]
         for h, part in enumerate(butterfly(parts)):
-            middle_ref[h, LOW * low : LOW * (low + 1), :] = part.astype(jnp.bfloat16)
+            lanes = slice(h % WIDE * cols, (h % WIDE + 1) * cols)
+            middle_ref[h // WIDE, LOW * low : LOW * (low + 1), lanes] = part
 
     refs = (even_ref, odd_ref)
     for low in range(LOW):
         prepare(0, low, even_ref)
     largest = jnp.zeros((LOW, cols), jnp.bfloat16)
     for group in range(groups):
-        for h in range(HIGH):
-            product = jnp.dot(table, refs[group % 2][h], preferred_element_type=jnp.float32)
+        for first in range(0, HIGH, WIDE):
+            product = jnp.dot(table, refs[group % 2][first // WIDE], preferred_element_type=jnp.float32)
             if group + 1 < groups:
-                for low in (2 * h, 2 * h + 1):
+                for low in range(first * LOW // HIGH, (first + WIDE) * LOW // HIGH):
                     prepare(group + 1, low, refs[(group + 1) % 2])
             for low in range(LOW):
-                p = device_at(h * LOW + low)
-                part = (product[LOW * low : LOW * (low + 1), :] * factor_ref[p : p + 1, :]).astype(jnp.bfloat16)
-                largest = jnp.maximum(largest, jnp.abs(part))
-                stage_ref[group, p] = part
-        write(group).start()
+                for h in range(first, first + WIDE):
+                    p = h * LOW + low
+                    part = product[LOW * low : LOW * (low + 1), (h - first) * cols : (h - first + 1) * cols]
+                    part = (part * factor_ref[p : p + 1, :]).astype(jnp.bfloat16)
+                    largest = jnp.maximum(largest, jnp.abs(part))
+                    stage_ref[group, p] = part
+            if (first + WIDE) % WRITTEN == 0:
+                write(group, first + WIDE - WRITTEN).start()
 
     peak = jnp.max(largest.astype(jnp.float32), axis=(0, 1), keepdims=True)
     peak_ref[...] = jnp.broadcast_to(peak.reshape(1, 1, 1), peak_ref.shape)
     for group in range(groups):
-        write(group).wait()
+        for first in range(0, HIGH, WRITTEN):
+            write(group, first).wait()
 
 
 def after(exponents, received, devices):
@@ -152,9 +161,9 @@
         scratch_shapes=[
             pltpu.VMEM((outer, cols), jnp.float32),
             pltpu.VMEM((groups, outer, LOW, cols), jnp.bfloat16),
-            pltpu.VMEM((HIGH, LOW * LOW, cols), jnp.bfloat16),
-            pltpu.VMEM((HIGH, LOW * LOW, cols), jnp.bfloat16),
-            pltpu.SemaphoreType.DMA((groups,)),
+            pltpu.VMEM((HIGH // WIDE, LOW * LOW, WIDE * cols), jnp.bfloat16),
+            pltpu.VMEM((HIGH // WIDE, LOW * LOW, WIDE * cols), jnp.bfloat16),
+            pltpu.SemaphoreType.DMA((groups, HIGH // WRITTEN)),
         ],
         compiler_params=pltpu.CompilerParams(vmem_limit_bytes=VMEM_BYTES),
     )(exponents, pltpu.with_memory_space_constraint(received, pltpu.VMEM))
@@ -172,7 +181,7 @@
     received = exchange(packed)
     quantized, peaks = after(exponents.T, received, devices)
     shared = exchange(peaks)
-    return (quantized.reshape(OUTER * INNER, cols), jnp.max(shared))
+    return (quantized.reshape(OUTER * INNER, cols), jnp.max(shared.reshape(devices, 128)[:, :1]))
 
 
 def solution(mesh):

time: 133 us -> 132 us (level)
  no operation moved by 1% of the time
where the time goes in v6:
time: 132 us
  blocking collectives  123 us (93%)
  Pallas kernels  8.47 us (6%)
    all_to_all x1, blocking collectives, on_device(): received = exchange(packed)  108 us
    all_to_all x1, blocking collectives, on_device(): shared = exchange(peaks)  14.4 us
    pallas_call x1, Pallas kernels, after(): pl.pallas_call(after_kernel, out_shape=(jax.ShapeDtypeStruct((outer, inne...  4.66 us
    pallas_call x1, Pallas kernels, before(): pl.pallas_call(before_kernel, out_shape=pltpu.VMEM((devices, rows, total...  3.81 us

profile of v6, /device:TPU:1, one launch (start us, length us, event | category | flops | bytes accessed | tf_op | source)
XLA Modules:
  0.0 132.3 jit_solution(9932769846819639023)
XLA Ops:
  0.6 3.8 %shard_map.41 = bf16[128,128,256]{2,1,0:T(8,128)(2,1)S(1)} custom-call(bf16[128,32768]{1,0:T(8,128)(2,1)} %weights_ref.1), custom_call_target="tpu_custom_call" | custom-call | tf_op jit(solution)/shard_map/pallas_call | solution.py:90
  4.4 0.0 copy-start
  4.5 108.1 %all_to_all.10.received_ref = bf16[128,128,256]{2,1,0:T(8,128)(2,1)S(1)} all-to-all(bf16[128,128,256]{2,1,0:T(8,128)(2,1)S(1)} %shard_map.41), channel_id=1, replica_groups={{0,4,8,12,64,68,72,76,2,6,10,14,66,70,74,78,1,5,9,13,65,69,73,77,3,7,11..., dimensions={0} | all-to-all | bytes 16777216 | tf_op jit(solution)/shard_map/all_to_all | solution.py:181
  112.6 0.0 copy-done
  112.6 4.7 %shard_map.42 = (bf16[128,128,256]{2,1,0:T(8,128)(2,1)}, f32[128,1,128]{2,1,0:T(1,128)S(1)}) custom-call(s32[2,128]{1,0:T(2,128)S(1)} %bitcast.3, bf16[128,128,256]{2,1,0:T(8,128)(2,1)S(1)} %all_to_all.10.received_ref), custom_call_target="tpu_custom_call" | custom-call | tf_op jit(solution)/shard_map/pallas_call | solution.py:153
  117.3 14.4 %all_to_all.11 = f32[128,1,128]{2,1,0:T(1,128)S(1)} all-to-all(f32[128,1,128]{2,1,0:T(1,128)S(1)} %get-tuple-element.5), channel_id=1, replica_groups={{0,4,8,12,64,68,72,76,2,6,10,14,66,70,74,78,1,5,9,13,65,69,73,77,3,7,11..., dimensions={0} | all-to-all | bytes 131072 | tf_op jit(solution)/shard_map/all_to_all | solution.py:183
  131.7 0.6 slice_reduce_fusion
Async XLA Ops:
  4.4 108.1 %copy-start = (s32[128,2]{0,1:T(2,128)S(1)}, s32[128,2]{0,1:T(2,128)}, u32[]{:S(2)}) copy-start(s32[128,2]{0,1:T(2,128)} %param.3) | copy-start | bytes 3076

commit v7 on v6

--- a/solution.py
+++ b/solution.py
@@ -18,7 +18,7 @@
 PIECES = 16
 WIDE = 2
 WRITTEN = 4
-EXCHANGE_BITS = (5, 4, 0, 1, 6, 3, 2)
+EXCHANGE_BITS = (5, 4, 0, 3, 2, 1, 6)
 
 VMEM_BYTES = 20 * 1024 * 1024
 

time: 132 us -> 132 us (level)
  no operation moved by 1% of the time
where the time goes in v7:
time: 132 us
  blocking collectives  123 us (93%)
  Pallas kernels  8.46 us (6%)
    all_to_all x1, blocking collectives, on_device(): received = exchange(packed)  109 us
    all_to_all x1, blocking collectives, on_device(): shared = exchange(peaks)  13.6 us
    pallas_call x1, Pallas kernels, after(): pl.pallas_call(after_kernel, out_shape=(jax.ShapeDtypeStruct((outer, inne...  4.65 us
    pallas_call x1, Pallas kernels, before(): pl.pallas_call(before_kernel, out_shape=pltpu.VMEM((devices, rows, total...  3.81 us

profile of v7, /device:TPU:1, one launch (start us, length us, event | category | flops | bytes accessed | tf_op | source)
XLA Modules:
  0.0 132.3 jit_solution(4665278577309902077)
XLA Ops:
  0.6 3.8 %shard_map.41 = bf16[128,128,256]{2,1,0:T(8,128)(2,1)S(1)} custom-call(bf16[128,32768]{1,0:T(8,128)(2,1)} %weights_ref.1), custom_call_target="tpu_custom_call" | custom-call | tf_op jit(solution)/shard_map/pallas_call | solution.py:90
  4.4 0.0 copy-start
  4.5 109.0 %all_to_all.10.received_ref = bf16[128,128,256]{2,1,0:T(8,128)(2,1)S(1)} all-to-all(bf16[128,128,256]{2,1,0:T(8,128)(2,1)S(1)} %shard_map.41), channel_id=1, replica_groups={{0,64,2,66,4,68,6,70,8,72,10,74,12,76,14,78,1,65,3,67,5,69,7,71,9,73,11..., dimensions={0} | all-to-all | bytes 16777216 | tf_op jit(solution)/shard_map/all_to_all | solution.py:181
  113.4 0.0 copy-done
  113.4 4.7 %shard_map.42 = (bf16[128,128,256]{2,1,0:T(8,128)(2,1)}, f32[128,1,128]{2,1,0:T(1,128)S(1)}) custom-call(s32[2,128]{1,0:T(2,128)S(1)} %bitcast.3, bf16[128,128,256]{2,1,0:T(8,128)(2,1)S(1)} %all_to_all.10.received_ref), custom_call_target="tpu_custom_call" | custom-call | tf_op jit(solution)/shard_map/pallas_call | solution.py:153
  118.1 13.6 %all_to_all.11 = f32[128,1,128]{2,1,0:T(1,128)S(1)} all-to-all(f32[128,1,128]{2,1,0:T(1,128)S(1)} %get-tuple-element.5), channel_id=1, replica_groups={{0,64,2,66,4,68,6,70,8,72,10,74,12,76,14,78,1,65,3,67,5,69,7,71,9,73,11..., dimensions={0} | all-to-all | bytes 131072 | tf_op jit(solution)/shard_map/all_to_all | solution.py:183
  131.6 0.6 slice_reduce_fusion
Async XLA Ops:
  4.4 109.0 %copy-start = (s32[128,2]{0,1:T(2,128)S(1)}, s32[128,2]{0,1:T(2,128)}, u32[]{:S(2)}) copy-start(s32[128,2]{0,1:T(2,128)} %param.3) | copy-start | bytes 3076

commit v8 on v7

--- a/solution.py
+++ b/solution.py
@@ -18,7 +18,7 @@
 PIECES = 16
 WIDE = 2
 WRITTEN = 4
-EXCHANGE_BITS = (5, 4, 0, 3, 2, 1, 6)
+EXCHANGE_BITS = (1, 6, 0, 5, 4, 3, 2)
 
 VMEM_BYTES = 20 * 1024 * 1024
 

time: 132 us -> 133 us (level)
    all_to_all x1, blocking collectives: 13.6 us -> 14.9 us  [on_device(): shared = exchange(peaks)]
where the time goes in v8:
time: 133 us; the launch traced here: 132 us
  blocking collectives  123 us (92%)
  Pallas kernels  8.47 us (6%)
    all_to_all x1, blocking collectives, on_device(): received = exchange(packed)  108 us
    all_to_all x1, blocking collectives, on_device(): shared = exchange(peaks)  14.9 us
    pallas_call x1, Pallas kernels, after(): pl.pallas_call(after_kernel, out_shape=(jax.ShapeDtypeStruct((outer, inne...  4.66 us
    pallas_call x1, Pallas kernels, before(): pl.pallas_call(before_kernel, out_shape=pltpu.VMEM((devices, rows, total...  3.81 us

profile of v8, /device:TPU:1, one launch (start us, length us, event | category | flops | bytes accessed | tf_op | source)
XLA Modules:
  0.0 132.4 jit_solution(4097089314797860856)
XLA Ops:
  0.6 3.8 %shard_map.41 = bf16[128,128,256]{2,1,0:T(8,128)(2,1)S(1)} custom-call(bf16[128,32768]{1,0:T(8,128)(2,1)} %weights_ref.1), custom_call_target="tpu_custom_call" | custom-call | tf_op jit(solution)/shard_map/pallas_call | solution.py:90
  4.4 0.0 copy-start
  4.5 107.8 %all_to_all.10.received_ref = bf16[128,128,256]{2,1,0:T(8,128)(2,1)S(1)} all-to-all(bf16[128,128,256]{2,1,0:T(8,128)(2,1)S(1)} %shard_map.41), channel_id=1, replica_groups={{0,4,8,12,16,20,24,28,32,36,40,44,48,52,56,60,1,5,9,13,17,21,25,29,33,3..., dimensions={0} | all-to-all | bytes 16777216 | tf_op jit(solution)/shard_map/all_to_all | solution.py:181
  112.2 0.0 copy-done
  112.2 4.7 %shard_map.42 = (bf16[128,128,256]{2,1,0:T(8,128)(2,1)}, f32[128,1,128]{2,1,0:T(1,128)S(1)}) custom-call(s32[2,128]{1,0:T(2,128)S(1)} %bitcast.3, bf16[128,128,256]{2,1,0:T(8,128)(2,1)S(1)} %all_to_all.10.received_ref), custom_call_target="tpu_custom_call" | custom-call | tf_op jit(solution)/shard_map/pallas_call | solution.py:153
  116.9 14.9 %all_to_all.11 = f32[128,1,128]{2,1,0:T(1,128)S(1)} all-to-all(f32[128,1,128]{2,1,0:T(1,128)S(1)} %get-tuple-element.5), channel_id=1, replica_groups={{0,4,8,12,16,20,24,28,32,36,40,44,48,52,56,60,1,5,9,13,17,21,25,29,33,3..., dimensions={0} | all-to-all | bytes 131072 | tf_op jit(solution)/shard_map/all_to_all | solution.py:183
  131.8 0.6 slice_reduce_fusion
Async XLA Ops:
  4.4 107.8 %copy-start = (s32[128,2]{0,1:T(2,128)S(1)}, s32[128,2]{0,1:T(2,128)}, u32[]{:S(2)}) copy-start(s32[128,2]{0,1:T(2,128)} %param.3) | copy-start | bytes 3076
